TPU v7x, 32 devices: a whole 2x2x4 slice. The times are simulated.
32 devices in a mesh: dp: 2 (over core), expert: 16 (over z, y, x).
Axes of the slice: x: 2, y: 2, z: 4, core: 2. Of those that a mesh axis runs over, the one named last changes fastest.
Arguments:
- inputs: bfloat16 [32768, 512], P(('dp', 'expert')), may hold values from -6 to 6
- w_first: bfloat16 [16, 512, 256], P('expert'), may hold values from -0.25 to 0.25
- b_first: bfloat16 [16, 256], P('expert'), may hold values from -0.59765625 to 0.59765625
- w_second: bfloat16 [16, 256, 128], P('expert'), may hold values from -0.5 to 0.5
- b_second: bfloat16 [16, 128], P('expert'), may hold values from -0.59765625 to 0.59765625
- gate_weight: bfloat16 [2, 512, 16], replicated, may hold values from -0.125 to 0.125
- gate_bias: bfloat16 [2, 16], replicated, may hold values from -0.29882812 to 0.29882812
- tower_first_weight: bfloat16 [2, 128, 64], replicated, may hold values from -1 to 1
- tower_first_bias: bfloat16 [2, 64], replicated, may hold values from -0.59765625 to 0.59765625
- tower_last: bfloat16 [2, 64], replicated, may hold values from -1.5 to 1.5
- tower_out_bias: bfloat16 [2], replicated, may hold values from -2 to 2
- labels: int32 [2, 32768], P(None, ('dp', 'expert')), may hold values 0 or 1
- group_len: int32 [16], replicated, may hold values from 1 to 2048, as said below
- group_shard: int32 [16], replicated, may hold values from 0 to 1, as said below
Outputs:
- predictions: float32 [2, 32768], P(None, ('dp', 'expert'))
- input_grad: float32 [32768, 512], P(('dp', 'expert'))
- grad_w_first: float32 [16, 512, 256], P('expert')
- grad_b_first: float32 [16, 256], P('expert')
- grad_w_second: float32 [16, 256, 128], P('expert')
- grad_b_second: float32 [16, 128], P('expert')
- grad_gate: float32 [2, 512, 16], replicated
- grad_gate_bias: float32 [2, 16], replicated
- grad_tower_first: float32 [2, 128, 64], replicated
- grad_tower_bias: float32 [2, 64], replicated
- grad_tower_last: float32 [2, 64], replicated
- grad_tower_out_bias: float32 [2], replicated
Inputs may be any that keep to these rules, and one draw needn't show every extreme that they name: `group_len`: the lengths of the groups of one batch shard sum to at most 16384, and in every draw some shard's groups fill exactly 16384 slots. `group_shard`: each shard number is taken by exactly 8 groups.
All inputs are finite; a program needn't handle non-finite values. No bound on the sum of `labels` on one device may be relied on, other than what follows from the above.
Results may differ from a plain program's by a relative error of at most 0.0083.
Values may be sent and summed in bfloat16 or wider, within the bound.
No kernel may reach another device: no remote copies, remote signals or barrier semaphores. Data moves between devices by JAX's collectives and lax.ppermute only.
A program may use at most 320 MiB of HBM per device.

v0:
```python
import jax
import jax.numpy as jnp
from jax import lax
from jax.sharding import PartitionSpec as P


def row_weights(group_len, group_shard, shard, first, count):
    mine = group_shard == shard
    sizes = jnp.where(mine, group_len, 0)
    starts = jnp.cumsum(sizes) - sizes
    slots = (first + jnp.arange(count, dtype=jnp.int32))[:, None]
    inside = mine[None, :] & (slots >= starts[None, :]) & (slots < (starts + sizes)[None, :])
    recip = 1.0 / group_len.astype(jnp.float32)
    return jnp.sum(jnp.where(inside, recip[None, :], jnp.float32(0.0)), axis=1)


def gelu_back(value, grad):
    return jax.vjp(jax.nn.gelu, value)[1](grad)[0]


def per_device(
    inputs,
    w_first,
    b_first,
    w_second,
    b_second,
    gate_weight,
    gate_bias,
    tower_first_weight,
    tower_first_bias,
    tower_last,
    tower_out_bias,
    labels,
    group_len,
    group_shard,
):
    high_precision = lax.Precision.HIGHEST
    single_float32 = jnp.float32
    brain_float16 = jnp.bfloat16
    rows = inputs.shape[0]
    experts = lax.axis_size("expert")
    place = lax.axis_index("expert")
    weights = row_weights(group_len, group_shard, lax.axis_index("dp"), place * rows, rows)
    gate_logits = (
        jnp.einsum("rd,tde->tre", inputs, gate_weight, preferred_element_type=single_float32)
        + gate_bias.astype(single_float32)[:, None, :]
    )
    gate_probabilities = jax.nn.softmax(gate_logits, axis=-1)
    probabilities_reduced = gate_probabilities.astype(brain_float16)
    gathered, all_first = (
        lax.all_gather(inputs, "expert", axis=0, tiled=True),
        lax.all_gather(w_first, "expert", axis=0, tiled=True),
    )
    pre_one = jnp.dot(gathered, w_first[0], preferred_element_type=single_float32) + b_first[
        0
    ].astype(single_float32)
    hidden = jax.nn.gelu(pre_one).astype(brain_float16)
    pre_two = jnp.dot(hidden, w_second[0], preferred_element_type=single_float32) + b_second[
        0
    ].astype(single_float32)
    produced = jax.nn.gelu(pre_two).astype(brain_float16).reshape(experts, rows, pre_two.shape[1])
    expert_output = lax.all_to_all(produced, "expert", split_axis=0, concat_axis=0, tiled=True)
    mixed_experts = jnp.einsum(
        "kvy,yvo->kvo", probabilities_reduced, expert_output, preferred_element_type=single_float32
    ).astype(brain_float16)
    tower_preactivation = (
        jnp.einsum(
            "wmn,wnl->wml", mixed_experts, tower_first_weight, preferred_element_type=single_float32
        )
        + tower_first_bias.astype(single_float32)[:, None, :]
    )
    tower_act = jax.nn.gelu(tower_preactivation)
    last_f = tower_last.astype(single_float32)
    score = (
        jnp.einsum("trh,th->tr", tower_act, last_f, precision=high_precision)
        + tower_out_bias.astype(single_float32)[:, None]
    )
    predictions = jax.nn.sigmoid(score)
    d_score = weights[None, :] * (predictions - labels.astype(single_float32))
    grad_last = jnp.einsum("tr,trh->th", d_score, tower_act, precision=high_precision)
    grad_out_bias = jnp.sum(d_score, axis=1)
    tower_gradient = gelu_back(
        tower_preactivation, d_score[:, :, None] * last_f[:, None, :]
    ).astype(brain_float16)
    first_gradient = jnp.einsum(
        "ndw,ndx->nwx", mixed_experts, tower_gradient, preferred_element_type=single_float32
    )
    grad_bias = jnp.sum(tower_gradient.astype(single_float32), axis=1)
    mixed_gradient = jnp.einsum(
        "zwv,zcv->zwc", tower_gradient, tower_first_weight, preferred_element_type=single_float32
    )
    probability_gradient = jnp.einsum(
        "xin,ain->xia",
        mixed_gradient,
        expert_output.astype(single_float32),
        precision=high_precision,
    )
    output_gradient = jnp.einsum(
        "nic,nig->cig",
        probabilities_reduced.astype(single_float32),
        mixed_gradient,
        precision=high_precision,
    ).astype(brain_float16)
    d_gate = (
        gate_probabilities
        * (
            probability_gradient
            - jnp.sum(gate_probabilities * probability_gradient, axis=-1, keepdims=True)
        )
    ).astype(brain_float16)
    grad_gate = jnp.einsum("rd,tre->tde", inputs, d_gate, preferred_element_type=single_float32)
    grad_gate_bias = jnp.sum(d_gate.astype(single_float32), axis=1)
    input_grad = jnp.einsum(
        "tre,tde->rd", d_gate, gate_weight, preferred_element_type=single_float32
    )
    returned = lax.all_to_all(
        output_gradient, "expert", split_axis=0, concat_axis=0, tiled=True
    ).reshape(experts * rows, output_gradient.shape[2])
    d_two = gelu_back(pre_two, returned.astype(single_float32)).astype(brain_float16)
    contract_rows = (((0,), (0,)), ((), ()))
    contract_cols = (((1,), (1,)), ((), ()))
    grad_w_two = lax.dot_general(
        hidden, d_two, contract_rows, preferred_element_type=single_float32
    )
    grad_b_two = jnp.sum(d_two.astype(single_float32), axis=0)
    d_hidden = lax.dot_general(
        d_two, w_second[0], contract_cols, preferred_element_type=single_float32
    )
    d_one = gelu_back(pre_one, d_hidden).astype(brain_float16)
    grad_w_one = lax.dot_general(
        gathered, d_one, contract_rows, preferred_element_type=single_float32
    )
    grad_b_one = jnp.sum(d_one.astype(single_float32), axis=0)
    back_one = lax.all_to_all(
        d_one.reshape(experts, rows, d_one.shape[1]),
        "expert",
        split_axis=0,
        concat_axis=0,
        tiled=True,
    )
    input_grad = input_grad + jnp.einsum(
        "erh,edh->rd", back_one, all_first, preferred_element_type=single_float32
    )
    expert_grads = (grad_w_one[None], grad_b_one[None], grad_w_two[None], grad_b_two[None])
    grad_w_one, grad_b_one, grad_w_two, grad_b_two = lax.psum(
        (expert_grads[0], expert_grads[1], expert_grads[2], expert_grads[3]), "dp"
    )
    shared = lax.psum(
        (grad_gate, grad_gate_bias, first_gradient, grad_bias, grad_last, grad_out_bias),
        ("dp", "expert"),
    )
    return (
        predictions,
        input_grad,
        grad_w_one,
        grad_b_one,
        grad_w_two,
        grad_b_two,
        shared[0],
        shared[1],
        shared[2],
        shared[3],
        shared[4],
        shared[5],
    )


def solution(mesh):
    in_specs = (
        P(("dp", "expert"), None),
        P("expert", None, None),
        P("expert", None),
        P("expert", None, None),
        P("expert", None),
        P(),
        P(),
        P(),
        P(),
        P(),
        P(),
        P(None, ("dp", "expert")),
        P(),
        P(),
    )
    out_specs = (
        P(None, ("dp", "expert")),
        P(("dp", "expert"), None),
        P("expert", None, None),
        P("expert", None),
        P("expert", None, None),
        P("expert", None),
        P(),
        P(),
        P(),
        P(),
        P(),
        P(),
    )
    return jax.shard_map(
        per_device, mesh=mesh, in_specs=in_specs, out_specs=out_specs, check_vma=False
    )
```

profile of v0, /device:TPU:0, one launch (start us, length us, event | category | flops | bytes accessed | tf_op | source)
XLA Modules:
  0.0 811.1 jit_solution(8199978541334261812)
XLA Ops:
  7.2 0.7 all-gather.3.cloned.1.call-update
  7.9 0.7 add.142
  8.6 0.7 bitcast_convert_fusion
  9.3 195.9 %all-gather.3.cloned.1.call-done = bf16[16384,512]{1,0:T(8,128)(2,1)} async-done(((bf16[1024,512]{1,0:T(8,128)(2,1)}), bf16[16384,512]{1,0:T(8,128)(2,1)}) %all-gather.3.cloned.1.call-update) | async-done | bytes 16777232 | tf_op jit(solution)/shard_map/all_gather | solution.py:51
  205.1 8.2 %convolution_add_fusion = f32[16384,256]{1,0:T(8,128)S(1)} fusion(bf16[16384,512]{1,0:T(8,128)(2,1)} %all-gather.3.cloned.1.call-done, f32[256]{0:T(256)S(1)} %bitcast.102, bf16[1,512,256]{2,1,0:T(8,128)(2,1)} %param.15), kind=kOutput, calls=%fused_computation.3 | convolution fusion | flops 4299161600 | bytes 33817600 | tf_op jit(solution)/shard_map/dot_general | solution.py:54
  213.4 10.9 %multiply_convert_fusion.1 = (bf16[16384,128]{1,0:T(8,128)(2,1)}, f32[16384,128]{1,0:T(8,128)}) fusion(f32[128]{0:T(128)S(1)} %bitcast_convert_fusion, bf16[1,256,128]{2,1,0:T(8,128)(2,1)S(1)} %copy-done, f32[16384,256]{1,0:T(8,128)S(1)} %convolution_add_fusion), kind=kOutput, calls=%fused_computation.29 | convolution fusion | flops 1132462080 | bytes 29426176 | tf_op jit(solution)/shard_map/dot_general | solution.py:58
  224.4 4.8 all-to-all-start
  229.3 0.5 fusion.78
  229.8 0.4 copy.61
  230.2 0.1 copy.63
  230.3 0.1 reduce
  230.5 0.1 select_reduce_fusion
  230.6 77.9 %all-to-all-done = bf16[16,1024,128]{2,1,0:T(8,128)(2,1)} async-done(((bf16[16,1024,128]{2,1,0:T(8,128)(2,1)}), bf16[16,1024,128]{2,1,0:T(8,128)(2,1)}, u32[]{:S(2)}, u32[]{:S(2)}) %all-to-all-start) | async-done | bytes 4194336 | tf_op jit(solution)/shard_map/all_to_all | solution.py:62
  308.6 5.0 fusion.25
  313.5 0.3 convolution_add_fusion.2
  313.9 0.4 fusion.50
  314.3 0.8 fusion.73
  315.1 0.5 convert_reduce_fusion.2
  315.6 0.7 copy-done.5
  316.3 0.4 fusion.81
  316.7 6.8 convert_bitcast_fusion
  323.5 1.1 copy.69
  324.6 113.2 %all_to_all.15 = bf16[16,1024,128]{2,1,0:T(8,128)(2,1)S(1)} all-to-all(bf16[16,1024,128]{2,1,0:T(8,128)(2,1)S(1)} %copy.69), channel_id=1, replica_groups=mesh['dp'=2,'expert'=16] {'expert'}, dimensions={0} | all-to-all | bytes 8388608 | tf_op jit(solution)/shard_map/all_to_all | solution.py:116
  437.8 7.5 convert_reduce_fusion.1
  445.4 15.3 %convert_reduce_fusion = (f32[256]{0:T(256)S(1)}, bf16[16384,256]{1,0:T(8,128)(2,1)}) fusion(f32[16384,256]{1,0:T(8,128)S(1)} %bitcast.97, bf16[16384,128]{1,0:T(8,128)(2,1)} %get-tuple-element.78, bf16[1,256,128]{2,1,0:T(8,128)(2,1)S(1)} %copy-done), kind=kOutput, calls=%fused_computation.12 | convolution fusion | flops 1166016256 | bytes 29426688 | tf_op jit(solution)/shard_map/dot_general | solution.py:126
  460.7 4.8 all-to-all-start.2
  465.5 0.0 all-reduce.9.cloned.1.call-start
  465.6 11.4 %convolution_bitcast_fusion.1 = f32[1,256,128]{2,1,0:T(8,128)} fusion(bf16[16384,128]{1,0:T(8,128)(2,1)} %get-tuple-element.78, f32[16384,256]{1,0:T(8,128)} %copy-done.3), kind=kOutput, calls=%fused_computation.44 | convolution fusion | flops 1111490560 | bytes 21102592 | tf_op jit(solution)/shard_map/dot_general | solution.py:122
  476.9 8.9 %convolution_bitcast_fusion = f32[1,512,256]{1,2,0:T(8,128)} fusion(bf16[16384,256]{1,0:T(8,128)(2,1)S(1)} %copy-done.2, bf16[16384,512]{1,0:T(8,128)(2,1)} %all-gather.3.cloned.1.call-done), kind=kOutput, calls=%fused_computation.39 | convolution fusion | flops 4294967296 | bytes 25690112 | tf_op jit(solution)/shard_map/dot_general | solution.py:130
  485.9 0.0 all-gather.5.cloned.1.call-start
  485.9 0.7 all-gather.5.cloned.1.call-update
  486.6 0.3 all-reduce.7.cloned.1.call-start
  486.9 14.2 %fusion.18 = f32[1024,16,2]{1,2,0:T(2,128)} fusion(bf16[16,1024,128]{2,1,0:T(8,128)(2,1)} %all-to-all-done, f32[2,1024,128]{2,1,0:T(8,128)S(1)} %fusion.81), kind=kOutput, calls=%fused_computation.31 | convolution fusion | flops 50331648 | bytes 5373952 | tf_op jit(solution)/shard_map/xin,ain->xia/dot_general | solution.py:92
  501.1 1.4 copy.66
  502.5 0.1 fusion.51
  502.5 0.1 convert_reduce_fusion.3
  502.7 1.9 fusion.45
  504.6 0.9 convolution_bitcast_fusion.2
  505.5 0.7 fusion.49
  506.2 205.0 %all-reduce = (f32[2,16]{1,0:T(2,128)}, f32[2,64]{1,0:T(2,128)}, f32[2,64]{1,0:T(2,128)}, f32[2]{0:T(128)}) all-reduce(f32[2,16]{1,0:T(2,128)S(1)} %get-tuple-element.75, f32[2,64]{1,0:T(2,128)S(1)} %get-tuple-element.73, f32[2,64]{1,0:T(2,128)S(1)} %bitcast.103, ...), channel_id=1, replica_groups=mesh['dp'=2,'expert'=16] {'dp','expert'}, use_global_device_ids=true, to_apply=%region_13.14 | all-reduce | flops 290 | bytes 2320 | tf_op jit(solution)/shard_map/psum | solution.py:148
  711.2 0.5 fusion.82
  711.7 3.0 all-reduce.2
  714.7 2.1 copy.71
  716.8 10.5 %bitcast_add_fusion = f32[1024,512]{1,0:T(8,128)} fusion(f32[1024,512,1]{1,0,2:T(8,128)S(1)} %fusion.82, bf16[16,1024,256]{2,1,0:T(8,128)(2,1)} %all-to-all-done.2, bf16[16,512,256]{2,1,0:T(8,128)(2,1)} %all-gather.5.cloned.1.call-done), kind=kOutput, calls=%fused_computation.35 | convolution fusion | flops 4295491584 | bytes 16777216 | tf_op jit(solution)/shard_map/erh,edh->rd/dot_general | solution.py:141
  727.3 73.3 %all-reduce.7.cloned.1.call-done = (f32[2,512,16]{1,2,0:T(8,128)}, f32[2,128,64]{1,2,0:T(8,128)}) async-done(((f32[2,512,16]{1,2,0:T(8,128)}, f32[2,128,64]{1,2,0:T(8,128)}), (f32[2,512,16]{1,2,0:T(8,128)}, f32[2,128,64]{1,2,0:T(8,128)})) %all-reduce.7.cloned.1.call-update) | async-done | bytes 131088 | tf_op jit(solution)/shard_map/psum | solution.py:148
  800.5 0.7 copy.102
  801.2 1.5 copy.103
  802.7 1.5 copy.104
  (65 shorter events, 0.3 us)
Async XLA Ops:
  7.2 206.2 %copy-start = (bf16[1,256,128]{2,1,0:T(8,128)(2,1)S(1)}, bf16[1,256,128]{2,1,0:T(8,128)(2,1)}, u32[]{:S(2)}) copy-start(bf16[1,256,128]{2,1,0:T(8,128)(2,1)} %param.17) | copy-start | bytes 196612
  7.2 198.0 %all-gather.3.cloned.1.call-start = ((), (), s32[]{:S(2)}) async-start(), calls=%async_computation.3 | async-start | bytes 17825792 | tf_op jit(solution)/shard_map/all_gather | solution.py:51
  213.4 10.9 %copy-start.3 = (f32[16384,256]{1,0:T(8,128)}, f32[16384,256]{1,0:T(8,128)S(1)}, u32[]{:S(2)}) copy-start(f32[16384,256]{1,0:T(8,128)S(1)} %convolution_add_fusion) | copy-start | bytes 50331652
  224.3 5.0 copy-start.14
  224.3 5.0 copy-start.4
  224.3 5.0 copy-start.8
  224.3 5.9 copy-start.15
  224.3 5.9 copy-start.12
  224.3 5.9 copy-start.13
  224.3 6.1 copy-start.16
  224.3 6.1 copy-start.17
  224.4 89.2 %copy-start.10 = (bf16[2,128,64]{1,2,0:T(8,128)(2,1)S(1)}, bf16[2,128,64]{1,2,0:T(8,128)(2,1)}, u32[]{:S(2)}) copy-start(bf16[2,128,64]{1,2,0:T(8,128)(2,1)} %param.21) | copy-start | bytes 98308
  224.4 89.9 %copy-start.11 = (s32[2,1024]{1,0:T(2,128)S(1)}, s32[2,1024]{1,0:T(2,128)}, u32[]{:S(2)}) copy-start(s32[2,1024]{1,0:T(2,128)} %param.25) | copy-start | bytes 24580
  224.4 84.2 %all-to-all-start = ((bf16[16,1024,128]{2,1,0:T(8,128)(2,1)}), bf16[16,1024,128]{2,1,0:T(8,128)(2,1)}, u32[]{:S(2)}, u32[]{:S(2)}) async-start(bf16[16,1024,128]{2,1,0:T(8,128)(2,1)} %bitcast.100), calls=%async_computation | async-start | bytes 8388608 | tf_op jit(solution)/shard_map/all_to_all | solution.py:62
  313.5 3.1 copy-start.7
  315.6 0.7 copy-start.5
  316.7 121.1 %slice-start.4 = ((s8[8388608]{0:T(1024)(128)(4,1)}), s8[4194304]{0:T(1024)(128)(4,1)S(1)}, s32[]{:S(2)}) async-start(s8[8388608]{0:T(1024)(128)(4,1)} %bitcast.98), calls=%async_computation.11 | async-start | bytes 8388608
  323.5 114.3 %slice-start.5 = ((s8[8388608]{0:T(1024)(128)(4,1)}), s8[4194304]{0:T(1024)(128)(4,1)S(1)}, s32[]{:S(2)}) async-start(s8[8388608]{0:T(1024)(128)(4,1)} %bitcast.98), calls=%async_computation.12 | async-start | bytes 8388608
  323.5 121.9 %slice-start = ((s8[16777216]{0:T(1024)(128)(4,1)}), s8[4194304]{0:T(1024)(128)(4,1)S(1)}, s32[]{:S(2)}) async-start(s8[16777216]{0:T(1024)(128)(4,1)} %bitcast.96), calls=%async_computation.7 | async-start | bytes 8388608
  324.6 120.8 %slice-start.1 = ((s8[16777216]{0:T(1024)(128)(4,1)}), s8[4194304]{0:T(1024)(128)(4,1)S(1)}, s32[]{:S(2)}) async-start(s8[16777216]{0:T(1024)(128)(4,1)} %bitcast.96), calls=%async_computation.8 | async-start | bytes 8388608
  437.8 7.5 slice-start.2
  437.8 7.5 slice-start.3
  460.7 256.0 %all-to-all-start.2 = ((bf16[16,1024,256]{2,1,0:T(8,128)(2,1)}), bf16[16,1024,256]{2,1,0:T(8,128)(2,1)}, u32[]{:S(2)}, u32[]{:S(2)}) async-start(bf16[16,1024,256]{2,1,0:T(8,128)(2,1)} %bitcast.95), calls=%async_computation.2 | async-start | bytes 16777216 | tf_op jit(solution)/shard_map/all_to_all | solution.py:134
  465.5 249.2 %all-reduce.9.cloned.1.call-start = ((), (), s32[]{:S(2)}) async-start(), calls=%async_computation.6 | async-start | bytes 1310720 | tf_op jit(solution)/shard_map/psum | solution.py:145
  465.5 11.4 %copy-start.2 = (bf16[16384,256]{1,0:T(8,128)(2,1)S(1)}, bf16[16384,256]{1,0:T(8,128)(2,1)}, u32[]{:S(2)}) copy-start(bf16[16384,256]{1,0:T(8,128)(2,1)} %get-tuple-element.86) | copy-start | bytes 25165828
  485.9 16.8 %copy-start.6 = (bf16[2,1024,64]{1,2,0:T(8,128)(2,1)S(1)}, bf16[2,1024,64]{1,2,0:T(8,128)(2,1)}, u32[]{:S(2)}) copy-start(bf16[2,1024,64]{1,2,0:T(8,128)(2,1)} %copy-done.5) | copy-start | bytes 786436
  485.9 230.9 %all-gather.5.cloned.1.call-start = ((), (), s32[]{:S(2)}) async-start(), calls=%async_computation.4 | async-start | bytes 4456448 | tf_op jit(solution)/shard_map/all_gather | solution.py:52
  486.6 313.9 %all-reduce.7.cloned.1.call-start = ((), (), s32[]{:S(2)}) async-start(), calls=%async_computation.5 | async-start | bytes 262144 | tf_op jit(solution)/shard_map/psum | solution.py:148
  714.7 89.4 %copy-start.1 = (bf16[1,256,128]{2,1,0:T(8,128)(2,1)S(1)}, bf16[1,256,128]{2,1,0:T(8,128)(2,1)}, u32[]{:S(2)}) copy-start(bf16[1,256,128]{2,1,0:T(8,128)(2,1)} %param.17) | copy-start | bytes 196612
  716.8 83.8 %copy-start.9 = (f32[1,256,128]{2,1,0:T(8,128)S(1)}, f32[1,256,128]{2,1,0:T(8,128)}, u32[]{:S(2)}) copy-start(f32[1,256,128]{2,1,0:T(8,128)} %get-tuple-element.91) | copy-start | bytes 393220
Sparse Core Ops, SparseCore 0:
  10.8 194.3 all-gather.2
  486.0 20.2 all-reduce.8
  509.5 163.2 all-gather.4
  680.4 120.0 all-reduce.6
where the time goes:
time: 815 us; the launch traced here: 811 us
  waiting for transfers between devices  348 us (43%)
  blocking collectives  321 us (39%)
  matrix products  96.7 us (12%)
  between operations  14.6 us (2%)
  other arithmetic  10.6 us (1%)
  starting transfers between devices  10 us (1%)
  local copies, waits for them, and re-layouts  9.44 us (1%)
    psum x1, blocking collectives, per_device(): lax.psum((grad_gate, grad_gate_bias, first_gradient, grad_bias, grad_last...  205 us
    all_gather x1, waiting for transfers between devices, per_device(): lax.all_gather(inputs, 'expert', axis=0, tiled=True)  196 us
    all_to_all x1, blocking collectives, per_device(): lax.all_to_all(output_gradient, 'expert', split_axis=0, concat_axis=0, ti...  113 us
    all_to_all x1, waiting for transfers between devices, per_device(): lax.all_to_all(produced, 'expert', split_axis=0, concat_axis=0, tiled=True)  77.9 us
    psum x1, waiting for transfers between devices, per_device(): lax.psum((grad_gate, grad_gate_bias, first_gradient, grad_bias, grad_last...  73.3 us
  transfers between devices with their start and end apart: 6, of which 3 were waited for; matrix products, arithmetic and copies ran while one was open for 7% of the time, Pallas kernels for 0%

commit v1 on v0

v1 whole, which is shorter than its diff:
```python
import functools

import jax
import jax.numpy as jnp
from jax import lax
from jax.experimental import pallas as pl
from jax.experimental.pallas import tpu as pltpu
from jax.sharding import PartitionSpec as P

F32 = jnp.float32
BF16 = jnp.bfloat16
VMEM_BYTES = 56 * 2**20
CHUNK = 512
ROOT = 0.7978845608028654
CUBE = 0.044715
NN = (((1,), (0,)), ((), ()))
NT = (((1,), (1,)), ((), ()))
TN = (((0,), (0,)), ((), ()))
BIAS_ROWS = 16

def dot(a, b, dims):
    return lax.dot_general(a, b, dims, preferred_element_type=F32)

def gelu_pair(v):
    square = v * v
    upper = 0.5 + 0.5 * jnp.tanh(v * (ROOT + (ROOT * CUBE) * square))
    value = v * upper
    slope = upper + value * (1.0 - upper) * (2.0 * ROOT + (6.0 * ROOT * CUBE) * square)
    return value, slope

def row_weights(group_len, group_shard, shard, first, count):
    mine = group_shard == shard
    sizes = jnp.where(mine, group_len, 0)
    starts = jnp.cumsum(sizes) - sizes
    slots = (first + jnp.arange(count, dtype=jnp.int32))[:, None]
    inside = mine[None, :] & (slots >= starts[None, :]) & (slots < (starts + sizes)[None, :])
    recip = 1.0 / group_len.astype(F32)
    return jnp.sum(jnp.where(inside, recip[None, :], F32(0.0)), axis=1)

def params(flops, traffic):
    return dict(
        compiler_params=pltpu.CompilerParams(vmem_limit_bytes=VMEM_BYTES),
        cost_estimate=pl.CostEstimate(flops=flops, bytes_accessed=traffic, transcendentals=0),
    )

def whole(shape):
    return pl.BlockSpec(shape, lambda *_: (0,) * len(shape))


def gate_kernel(experts, half, slot_ref, x_ref, gw_ref, gb_ref, prob_ref, low_ref, scratch):
    logits = dot(gw_ref[...], x_ref[...], NT) + gb_ref[...]
    for t in range(2):
        part = logits[t * experts : (t + 1) * experts]
        top = jnp.max(part, axis=0, keepdims=True)
        e = jnp.exp(part - top)
        scratch[t * experts : (t + 1) * experts, :] = e / jnp.sum(e, axis=0, keepdims=True)
    for j in range(half):
        for t in range(2):
            row = scratch[pl.ds(t * experts + slot_ref[j], 1), :]
            prob_ref[j, t : t + 1, :] = row
            low_ref[j, t : t + 1, :] = row.astype(BF16).astype(F32)

def gate(slots, x, gw, gb):
    rows = x.shape[0]
    half = slots.shape[0]
    experts = 2 * half
    shape = jax.ShapeDtypeStruct((half, 2, rows), F32)

    return pl.pallas_call(
        functools.partial(gate_kernel, experts, half),
        in_specs=[
            pl.BlockSpec(memory_space=pltpu.SMEM),
            pl.BlockSpec(memory_space=pltpu.VMEM),
            pl.BlockSpec(memory_space=pltpu.VMEM),
            pl.BlockSpec(memory_space=pltpu.VMEM),
        ],
        out_specs=[pl.BlockSpec(memory_space=pltpu.VMEM)] * 2,
        out_shape=[shape, shape],
        scratch_shapes=[pltpu.VMEM((2 * experts, rows), F32)],
        **params(4 * rows * 512 * experts, rows * 1024),
    )(slots, x, gw, gb)


def bias_columns(pay):
    flipped = pay[-BIAS_ROWS:, :].astype(F32).T
    return flipped[:256, 0:1], flipped[256:384, 0:1]

def second_weight(pay):
    return jnp.concatenate([pay[256:320, :256], pay[256:320, 256:]], axis=0)

def forward_kernel(first, x_ref, pay_ref, low_ref, *refs):
    if first:
        h_ref, g1_ref, o_ref, g2_ref, mix_ref = refs
    else:
        mix_in, h_ref, g1_ref, o_ref, g2_ref, mix_ref = refs
    j = pl.program_id(0)

    @pl.when(j == 0)
    def _():
        mix_ref[...] = jnp.zeros_like(mix_ref) if first else mix_in[...]

    pay = pay_ref[0]
    w1 = pay[:256]
    w2 = second_weight(pay)
    b1, b2 = bias_columns(pay)
    rows = x_ref.shape[0]
    for k in range(0, rows, CHUNK):
        at = slice(k, k + CHUNK)
        value, slope = gelu_pair(dot(w1, x_ref[at, :], NT) + b1)
        hidden = value.astype(BF16)
        h_ref[0, :, at] = hidden
        g1_ref[0, :, at] = slope.astype(BF16)
        value, slope = gelu_pair(dot(w2, hidden, NN) + b2)
        out = value.astype(BF16)
        o_ref[0, :, at] = out
        g2_ref[0, :, at] = slope.astype(BF16)
        out = out.astype(F32)
        for t in range(2):
            mix_ref[t, :, at] += low_ref[0, t : t + 1, at] * out

def forward(x, pays, low, at, mixed):

    rows = x.shape[0]
    count = pays.shape[0]
    slot = lambda *shape: pl.BlockSpec((1,) + shape, lambda j: (j, 0, 0))
    mix_shape = (2, 128, rows)
    ins = [x, pays, low]
    specs = [whole(x.shape), slot(*pays.shape[1:]), pl.BlockSpec((1, 2, rows), lambda j: (at + j, 0, 0))]
    if mixed is not None:
        ins.append(mixed)
        specs.append(whole(mix_shape))
    return pl.pallas_call(
        functools.partial(forward_kernel, mixed is None),
        grid=(count,),
        in_specs=specs,
        out_specs=[slot(256, rows), slot(256, rows), slot(128, rows), slot(128, rows), whole(mix_shape)],
        out_shape=[
            jax.ShapeDtypeStruct((count, 256, rows), BF16),
            jax.ShapeDtypeStruct((count, 256, rows), BF16),
            jax.ShapeDtypeStruct((count, 128, rows), BF16),
            jax.ShapeDtypeStruct((count, 128, rows), BF16),
            jax.ShapeDtypeStruct(mix_shape, F32),
        ],
        **params(count * rows * (512 * 256 + 256 * 128) * 2, count * rows * 768 * 2),
    )(*ins)


def middle_kernel(
    experts,
    groups,
    slot_ref,
    x_ref,
    mix_ref,
    mix_other_ref,
    prob_ref,
    label_ref,
    weight_ref,
    tw_ref,
    tb_ref,
    tl_ref,
    to_ref,
    *refs,
):
    outs = refs[: len(groups)]
    pred_ref, dmix_ref, dgate_ref, shared_ref, mixed_low, d_tower, gates = refs[len(groups) :]
    rows = x_ref.shape[0]
    mine = rows // 2
    half = experts // 2
    gates[...] = jnp.zeros_like(gates)
    last = [jnp.zeros((64, 1), F32) for _ in range(2)]
    bias = [jnp.zeros((64, 1), F32) for _ in range(2)]
    out_bias = [jnp.zeros((1, 1), F32) for _ in range(2)]
    for k in range(0, rows, CHUNK):
        at = slice(k, k + CHUNK)
        other = slice((k + mine) % rows, (k + mine) % rows + CHUNK)
        d_mixed, centre = [], []
        for t in range(2):
            mixed = mix_ref[t, :, at] + mix_other_ref[t, :, other].astype(F32)
            low = mixed.astype(BF16)
            act, slope = gelu_pair(dot(tw_ref[t], low, NN) + tb_ref[t])
            score = jnp.sum(act * tl_ref[t], axis=0, keepdims=True) + to_ref[t]
            pred = 1.0 / (1.0 + jnp.exp(-score))
            pred_ref[t : t + 1, at] = pred
            d_score = weight_ref[:, at] * (pred - label_ref[t : t + 1, at].astype(F32))
            d_low = (d_score * tl_ref[t] * slope).astype(BF16)
            if k < mine:
                mixed_low[t, :, at] = low
                d_tower[t, :, at] = d_low
                last[t] = last[t] + jnp.sum(act * d_score, axis=1, keepdims=True)
                bias[t] = bias[t] + jnp.sum(d_low.astype(F32), axis=1, keepdims=True)
                out_bias[t] = out_bias[t] + jnp.sum(d_score, axis=1, keepdims=True)
            d_mixed.append(dot(tw_ref[t], d_low, TN))
            dmix_ref[t, :, at] = d_mixed[t]
            centre.append(jnp.sum(d_mixed[t] * mixed, axis=0, keepdims=True))
        j = 0
        for ref in outs:
            for i in range(ref.shape[0]):
                out = ref[i, :, at].astype(F32)
                for t in range(2):
                    d_prob = jnp.sum(d_mixed[t] * out, axis=0, keepdims=True)
                    d_gate = prob_ref[j, t : t + 1, at] * (d_prob - centre[t])
                    gates[pl.ds(t * experts + slot_ref[j], 1), at] = d_gate
                j += 1
    low = gates[...].astype(BF16)
    dgate_ref[...] = low
    for t in range(2):
        grad = dot(d_tower[t], mixed_low[t], NT)
        for k in range(4):
            shared_ref[16 * t : 16 * (t + 1), 128 * k : 128 * (k + 1)] = grad[16 * k : 16 * (k + 1)]
    shared_ref[32 : 32 + 2 * experts, :] = dot(low, x_ref[...], NN)
    tall = max(64, 2 * experts)
    pad = lambda col: jnp.concatenate([col, jnp.zeros((tall - col.shape[0], 1), F32)], axis=0) if col.shape[0] < tall else col
    columns = [
        pad(last[0]),
        pad(last[1]),
        pad(bias[0]),
        pad(bias[1]),
        jnp.broadcast_to(out_bias[0], (tall, 1)),
        jnp.broadcast_to(out_bias[1], (tall, 1)),
        pad(jnp.sum(low.astype(F32), axis=1, keepdims=True)),
    ]
    lane = lax.broadcasted_iota(jnp.int32, (tall, 128), 1)
    small = jnp.zeros((tall, 128), F32)
    for n, col in enumerate(columns):
        small = jnp.where(lane == n, jnp.broadcast_to(col, (tall, 128)), small)
    base = 32 + 2 * experts
    deep = tall // 4
    for k in range(4):
        shared_ref[base : base + deep, 128 * k : 128 * (k + 1)] = small[deep * k : deep * (k + 1)]

def middle(slots, x, mixed, mixed_other, prob, labels, weights, tw, tb, tl, to, outs):

    rows = x.shape[0]
    experts = 2 * slots.shape[0]
    shared_rows = 32 + 2 * experts + max(64, 2 * experts) // 4
    vmem = pl.BlockSpec(memory_space=pltpu.VMEM)
    smem = pl.BlockSpec(memory_space=pltpu.SMEM)
    return pl.pallas_call(
        functools.partial(middle_kernel, experts, tuple(o.shape[0] for o in outs)),
        in_specs=[smem] + [vmem] * 9 + [smem] + [vmem] * len(outs),
        out_specs=[vmem] * 4,
        out_shape=[
            jax.ShapeDtypeStruct((2, rows), F32),
            jax.ShapeDtypeStruct((2, 128, rows), F32),
            jax.ShapeDtypeStruct((2 * experts, rows), BF16),
            jax.ShapeDtypeStruct((shared_rows, 512), F32),
        ],
        scratch_shapes=[
            pltpu.VMEM((2, 128, rows // 2), BF16),
            pltpu.VMEM((2, 64, rows // 2), BF16),
            pltpu.VMEM((2 * experts, rows), F32),
        ],
        **params(rows * 128 * 64 * 12, rows * 128 * 2 * (experts // 2 + 8)),
    )(slots, x, mixed, mixed_other, prob, labels, weights, tw, tb, tl, to, *outs)


def backward_kernel(x_ref, pay_ref, low_ref, dmix_ref, h_ref, g1_ref, g2_ref, grad_ref, done_ref, d_two):
    w2 = second_weight(pay_ref[0])
    rows = x_ref.shape[0]
    sum_one = jnp.zeros((256, 128), F32)
    sum_two = jnp.zeros((128, 128), F32)
    for k in range(0, rows, CHUNK):
        at = slice(k, k + CHUNK)
        d_out = low_ref[0, 0:1, at] * dmix_ref[0, :, at] + low_ref[0, 1:2, at] * dmix_ref[1, :, at]
        two = d_out.astype(BF16).astype(F32) * g2_ref[0, :, at].astype(F32)
        two_low = two.astype(BF16)
        d_two[:, at] = two_low
        one = dot(w2, two_low, TN) * g1_ref[0, :, at].astype(F32)
        one_low = one.astype(BF16)
        done_ref[0, :, at] = one_low
        for n in range(0, CHUNK, 128):
            sum_one = sum_one + one[:, n : n + 128]
            sum_two = sum_two + two[:, n : n + 128]
    grad_ref[0, :256, :] = dot(done_ref[0], x_ref[...], NN).astype(BF16)
    second = dot(d_two[...], h_ref[0], NT).astype(BF16)
    grad_ref[0, 256:320, :256] = second[:64]
    grad_ref[0, 256:320, 256:] = second[64:]
    row = jnp.concatenate(
        [
            jnp.sum(sum_one.T, axis=0, keepdims=True),
            jnp.sum(sum_two.T, axis=0, keepdims=True),
            jnp.zeros((1, 128), F32),
        ],
        axis=1,
    )
    high = row.astype(BF16).astype(F32)
    index = lax.broadcasted_iota(jnp.int32, (BIAS_ROWS, 512), 0)
    both = jnp.where(index == 0, high, jnp.where(index == 1, row - high, 0.0))
    grad_ref[0, 320:, :] = both.astype(BF16)

def backward(x, pays, low, dmix, saved, at, first, count):
    h, g1, _, g2 = saved
    rows = x.shape[0]
    slot = lambda *shape: pl.BlockSpec((1,) + shape, lambda j: (first + j, 0, 0))
    out_slot = lambda *shape: pl.BlockSpec((1,) + shape, lambda j: (j, 0, 0))
    return pl.pallas_call(
        backward_kernel,
        grid=(count,),
        in_specs=[
            whole(x.shape),
            slot(*pays.shape[1:]),
            pl.BlockSpec((1, 2, rows), lambda j: (at + j, 0, 0)),
            whole(dmix.shape),
            slot(256, rows),
            slot(256, rows),
            slot(128, rows),
        ],
        out_specs=[out_slot(*pays.shape[1:]), out_slot(256, rows)],
        out_shape=[
            jax.ShapeDtypeStruct((count,) + pays.shape[1:], BF16),
            jax.ShapeDtypeStruct((count, 256, rows), BF16),
        ],
        scratch_shapes=[pltpu.VMEM((128, rows), BF16)],
        **params(count * rows * (512 * 256 + 2 * 256 * 128) * 2, count * rows * 900 * 2),
    )(x, pays, low, dmix, h, g1, g2)


def input_kernel(counts, add, dgate_ref, gw_ref, *refs):
    n = len(counts)
    total = dot(dgate_ref[...], gw_ref[...], TN)
    for ones, pays, count in zip(refs[:n], refs[n : 2 * n], counts):
        for j in range(count):
            total = total + dot(ones[j], pays[j, :256, :], TN)
    if add:
        total = total + refs[2 * n][...].astype(F32)
    refs[-1][...] = total.astype(refs[-1].dtype)

def input_gradient(dgate, gw, ones, pays, first, rows, added, dtype):

    block = 512
    start = first // block
    specs = [pl.BlockSpec((dgate.shape[0], block), lambda i: (0, start + i)), whole(gw.shape)]
    specs += [pl.BlockSpec((o.shape[0], 256, block), lambda i: (0, 0, start + i)) for o in ones]
    specs += [whole(p.shape) for p in pays]
    args = [dgate, gw, *ones, *pays]
    if added is not None:
        args.append(added)
        specs.append(pl.BlockSpec((block, 512), lambda i: (i, 0)))
    experts = sum(o.shape[0] for o in ones)
    return pl.pallas_call(
        functools.partial(input_kernel, tuple(o.shape[0] for o in ones), added is not None),
        grid=(rows // block,),
        in_specs=specs,
        out_specs=pl.BlockSpec((block, 512), lambda i: (i, 0)),
        out_shape=jax.ShapeDtypeStruct((rows, 512), dtype),
        **params(experts * rows * 512 * 256 * 2, experts * rows * 256 * 2),
    )(*args)


def per_device(
    inputs,
    w_first,
    b_first,
    w_second,
    b_second,
    gate_weight,
    gate_bias,
    tower_first_weight,
    tower_first_bias,
    tower_last,
    tower_out_bias,
    labels,
    group_len,
    group_shard,
):
    rows = inputs.shape[0]
    experts = lax.axis_size("expert")
    half = experts // 2
    bits = experts.bit_length() - 1
    core = lax.axis_index("dp")
    place = lax.axis_index("expert")
    owner = core == place // half

    order = [[bits - 2 - s for s in range(bits - 1)] for _ in range(2)]
    order[1][-2:] = order[1][-2:][::-1]

    def pairs(bit_of_core, want=None):
        return [
            (c * experts + q, c * experts + (q ^ (1 << bit_of_core[c])))
            for c in range(2)
            for q in range(experts)
            if want is None or (c == q // half) == want
        ]

    def send(value, bit_of_core, want=None):
        return lax.ppermute(value, ("dp", "expert"), pairs(bit_of_core, want))

    def swap(value):
        return lax.ppermute(value, "dp", [(0, 1), (1, 0)])

    masks = [
        [sum(((j >> s) & 1) << order[c][s] for s in range(bits - 1)) for j in range(half)]
        for c in range(2)
    ]
    mask = jnp.where(core == 0, jnp.array(masks[0], jnp.int32), jnp.array(masks[1], jnp.int32))
    slots = core * half + ((place % half) ^ mask)

    first_t = w_first[0].T
    second_t = w_second[0].T
    bias_row = jnp.concatenate([b_first[0], b_second[0], jnp.zeros((128,), BF16)])
    pay = jnp.concatenate(
        [
            first_t,
            jnp.concatenate([second_t[:64], second_t[64:]], axis=1),
            jnp.broadcast_to(bias_row[None], (BIAS_ROWS, 512)),
        ],
        axis=0,
    )
    top = [bits - 1] * 2
    low_bit = [order[0][0], order[1][0]]
    from_far = send(pay, top, True)
    from_near = send(pay, low_bit, True)
    x = jnp.concatenate([inputs, swap(inputs)], axis=0)
    label_pair = jnp.concatenate([labels, swap(labels)], axis=1)
    slot_zero = jnp.where(owner, pay, from_far)
    slot_one = from_near + send(slot_zero, low_bit, False)
    groups = [jnp.stack([slot_zero, slot_one])]
    for s in range(1, bits - 1):
        held = groups[0] if len(groups) == 1 else jnp.concatenate(groups, axis=0)
        groups.append(send(held, [order[0][s], order[1][s]]))
    starts = [0] + [1 << s for s in range(1, bits - 1)]

    gw = jnp.transpose(gate_weight, (0, 2, 1)).reshape(2 * experts, 512)
    gb = gate_bias.astype(F32).reshape(2 * experts, 1)
    prob, low = gate(slots, x, gw, gb)
    weights = jnp.concatenate(
        [
            row_weights(group_len, group_shard, core, place * rows, rows),
            row_weights(group_len, group_shard, 1 - core, place * rows, rows),
        ]
    )[None, :]

    mixed = None
    saved = []
    for at, group in zip(starts, groups):
        *kept, mixed = forward(x, group, low, at, mixed)
        saved.append(kept)

    mixed_other = swap(mixed.astype(BF16))
    predictions, dmix, dgate, shared = middle(
        slots,
        x,
        mixed,
        mixed_other,
        prob,
        label_pair,
        weights,
        jnp.transpose(tower_first_weight, (0, 2, 1)),
        tower_first_bias.astype(F32)[:, :, None],
        tower_last.astype(F32)[:, :, None],
        tower_out_bias.astype(F32),
        [kept[2] for kept in saved],
    )

    shared = shared + swap(shared)
    for b in reversed(range(bits)):
        shared = shared + send(shared, [b, b])

    grads = [None] * len(groups)
    ones = [None] * len(groups)
    coming = None
    for s in reversed(range(bits - 1)):
        g = max(s, 0)
        grads[g], ones[g] = backward(x, groups[g], low, dmix, saved[g], starts[g], 0, groups[g].shape[0])
        if s == 0:
            break
        total = grads[g]
        if coming is not None:
            size = total.shape[0]
            total = (total.astype(F32) + coming[size : 2 * size].astype(F32)).astype(BF16)
            coming = coming[:size]
        arrived = send(total, [order[0][s], order[1][s]])
        coming = arrived if coming is None else (coming.astype(F32) + arrived.astype(F32)).astype(BF16)
    total = grads[0].astype(F32) + coming.astype(F32)
    slot_zero, slot_one = total[0], total[1].astype(BF16)
    passed = slot_zero + send(slot_one, low_bit, False).astype(F32)
    far = send(passed.astype(BF16), top, False)
    near = send(slot_one, low_bit, True)
    final = slot_zero + far.astype(F32) + near.astype(F32)
    final = jnp.where(owner, final, swap(final))

    over = input_gradient(dgate, gw, ones, groups, rows, rows, None, BF16)
    input_grad = input_gradient(dgate, gw, ones, groups, 0, rows, swap(over), F32)

    grad_w_first = final[:256].T
    grad_w_second = jnp.concatenate([final[256:320, :256], final[256:320, 256:]], axis=0).T
    bias = final[320] + final[321]
    base = 32 + 2 * experts
    tall = max(64, 2 * experts)
    unfold = lambda block: jnp.concatenate([block[:, 128 * k : 128 * (k + 1)] for k in range(4)], axis=0)
    small = unfold(shared[base : base + tall // 4])
    tower_first = jnp.stack([unfold(shared[16 * t : 16 * (t + 1)]).T for t in range(2)])
    return (
        predictions[:, :rows],
        input_grad,
        grad_w_first[None],
        bias[None, :256],
        grad_w_second[None],
        bias[None, 256:384],
        jnp.transpose(shared[32:base].reshape(2, experts, 512), (0, 2, 1)),
        small[: 2 * experts, 6].reshape(2, experts),
        tower_first,
        small[:64, 2:4].T,
        small[:64, 0:2].T,
        small[0, 4:6],
    )

def solution(mesh):
    in_specs = (
        P(("dp", "expert"), None),
        P("expert", None, None),
        P("expert", None),
        P("expert", None, None),
        P("expert", None),
        P(),
        P(),
        P(),
        P(),
        P(),
        P(),
        P(None, ("dp", "expert")),
        P(),
        P(),
    )
    out_specs = (
        P(None, ("dp", "expert")),
        P(("dp", "expert"), None),
        P("expert", None, None),
        P("expert", None),
        P("expert", None, None),
        P("expert", None),
        P(),
        P(),
        P(),
        P(),
        P(),
        P(),
    )
    return jax.shard_map(
        per_device, mesh=mesh, in_specs=in_specs, out_specs=out_specs, check_vma=False
    )
```

time: 815 us -> 205 us (0.25)
  blocking collectives: 321 us -> 0 us
  waiting for transfers between devices: 348 us -> 44 us
  matrix products: 96.7 us -> 0 us
  Pallas kernels: 0 us -> 87.1 us
  starting transfers between devices: 10 us -> 43.7 us
  between operations: 14.6 us -> 1.13 us
    psum x2 -> x0, blocking collectives: 208 us -> none  [the longest x1 205 us: per_device(): lax.psum((grad_gate, grad_gate_bias, first_gradient, grad_bias, grad_last...]
    all_gather x2 -> x0, waiting for transfers between devices: 196 us -> none  [the longest x1 196 us: per_device(): lax.all_gather(inputs, 'expert', axis=0, tiled=True)]
    all_to_all x1 -> x0, blocking collectives: 113 us -> none  [per_device(): lax.all_to_all(output_gradient, 'expert', split_axis=0, concat_axis=0, ti...]
    dot_general x16 -> x0, matrix products: 96.3 us -> none  [the longest x1 15.3 us: per_device(): lax.dot_general(d_two, w_second[0], contract_cols, preferred_element_type...]
    pallas_call x0 -> x10, Pallas kernels: none -> 87.1 us  [the longest x3 36.1 us: forward(): pl.pallas_call(functools.partial(forward_kernel, mixed is None), grid=(co...]
    all_to_all x2 -> x0, waiting for transfers between devices: 77.9 us -> none  [the longest x1 77.9 us: per_device(): lax.all_to_all(produced, 'expert', split_axis=0, concat_axis=0, tiled=True)]
    psum x2 -> x0, waiting for transfers between devices: 73.3 us -> none  [the longest x1 73.3 us: per_device(): lax.psum((grad_gate, grad_gate_bias, first_gradient, grad_bias, grad_last...]
    ppermute x0 -> x20, waiting for transfers between devices: none -> 44 us  [the longest x14 44 us: send(): return lax.ppermute(value, ('dp', 'expert'), pairs(bit_of_core, want))]
  transfers between devices with their start and end apart: 6 -> 20, of which waited for: 3 -> 8; matrix products, arithmetic and copies ran while one was open for 7% -> 8% of each run, Pallas kernels for 0% -> 33%
where the time goes in v1:
time: 205 us; the launch traced here: 204 us
  Pallas kernels  87.1 us (42%)
  waiting for transfers between devices  44 us (21%)
  starting transfers between devices  43.7 us (21%)
  local copies, waits for them, and re-layouts  17.1 us (8%)
  other arithmetic  11.3 us (6%)
    ppermute x14, waiting for transfers between devices, send(): return lax.ppermute(value, ('dp', 'expert'), pairs(bit_of_core, want))  44 us
    pallas_call x3, Pallas kernels, forward(): pl.pallas_call(functools.partial(forward_kernel, mixed is None), grid=(co...  36.1 us
    ppermute x14, starting transfers between devices, send(): return lax.ppermute(value, ('dp', 'expert'), pairs(bit_of_core, want))  34.2 us
    pallas_call x3, Pallas kernels, backward(): pl.pallas_call(backward_kernel, grid=(count,), in_specs=[whole(x.shape),...  24.8 us
    pallas_call x2, Pallas kernels, input_gradient(): pl.pallas_call(functools.partial(input_kernel, tuple((o.shape[0] for o in...  13.4 us
    unnamed x39, local copies, waits for them, and re-layouts  9.71 us
    ppermute x6, starting transfers between devices, swap(): return lax.ppermute(value, 'dp', [(0, 1), (1, 0)])  9.46 us
    pallas_call x1, Pallas kernels, middle(): pl.pallas_call(functools.partial(middle_kernel, experts, tuple((o.shape[0...  9.45 us
  transfers between devices with their start and end apart: 20, of which 8 were waited for; matrix products, arithmetic and copies ran while one was open for 8% of the time, Pallas kernels for 33%

profile of v1, /device:TPU:0, one launch (start us, length us, event | category | flops | bytes accessed | tf_op | source)
XLA Modules:
  0.0 204.3 jit_solution(846099320790547415)
XLA Ops:
  0.6 0.9 copy.51
  1.6 1.1 copy.50
  2.7 0.7 reduce
  4.1 6.0 %collective-permute-start.1 = (bf16[336,512]{1,0:T(8,128)(2,1)S(1)}, bf16[336,512]{1,0:T(8,128)(2,1)S(1)}, u32[]{:S(2)}, u32[]{:S(2)}) collective-permute-start(bf16[336,512]{1,0:T(8,128)(2,1)S(1)} %pad_maximum_fusion.2), channel_id=1, source_target_pairs={{0,8},{1,9},{2,10},{3,11},{4,12},{5,13},{6,14},{7,15},{24,16},{25,... | collective-permute-start | bytes 1032200 | tf_op jit(solution)/shard_map/ppermute | solution.py:386
  10.1 3.5 %collective-permute-start.2 = (bf16[336,512]{1,0:T(8,128)(2,1)S(1)}, bf16[336,512]{1,0:T(8,128)(2,1)S(1)}, u32[]{:S(2)}, u32[]{:S(2)}) collective-permute-start(bf16[336,512]{1,0:T(8,128)(2,1)S(1)} %pad_maximum_fusion.2), channel_id=1, source_target_pairs={{0,4},{1,5},{2,6},{3,7},{4,0},{5,1},{6,2},{7,3},{24,28},{25,29},{2... | collective-permute-start | bytes 1032200 | tf_op jit(solution)/shard_map/ppermute | solution.py:386
  13.6 1.3 collective-permute-done.1
  14.9 0.7 collective-permute-start.3
  15.6 5.5 %collective-permute-done.2 = bf16[336,512]{1,0:T(8,128)(2,1)S(1)} collective-permute-done((bf16[336,512]{1,0:T(8,128)(2,1)S(1)}, bf16[336,512]{1,0:T(8,128)(2,1)S(1)}, u32[]{:S(2)}, u32[]{:S(2)}) %collective-permute-start.2) | collective-permute-done | bytes 344096 | tf_op jit(solution)/shard_map/ppermute | solution.py:386
  21.3 2.3 %collective-permute-start.4 = (bf16[2,336,512]{2,1,0:T(8,128)(2,1)S(1)}, bf16[2,336,512]{2,1,0:T(8,128)(2,1)S(1)}, u32[]{:S(2)}, u32[]{:S(2)}) collective-permute-start(bf16[2,336,512]{2,1,0:T(8,128)(2,1)S(1)} %pad_maximum_fusion.1.pay_ref.refs_3_), channel_id=1, source_target_pairs={{0,2},{1,3},{2,0},{3,1},{4,6},{5,7},{6,4},{7,5},{8,10},{9,11},{10,... | collective-permute-start | bytes 2064392 | tf_op jit(solution)/shard_map/ppermute | solution.py:386
  23.6 4.3 %collective-permute-start = (bf16[1024,512]{1,0:T(8,128)(2,1)}, bf16[1024,512]{1,0:T(8,128)(2,1)}, u32[]{:S(2)}, u32[]{:S(2)}) collective-permute-start(bf16[1024,512]{1,0:T(8,128)(2,1)} %param.16), channel_id=1, source_target_pairs={{0,16},{16,0},{1,17},{17,1},{2,18},{18,2},{3,19},{19,3},{4,20},{20... | collective-permute-start | bytes 3145736 | tf_op jit(solution)/shard_map/ppermute | solution.py:389
  27.9 4.6 %collective-permute-done.4.pay_ref.refs_4_ = bf16[2,336,512]{2,1,0:T(8,128)(2,1)S(1)} collective-permute-done((bf16[2,336,512]{2,1,0:T(8,128)(2,1)S(1)}, bf16[2,336,512]{2,1,0:T(8,128)(2,1)S(1)}, u32[]{:S(2)}, u32[]{:S(2)}) %collective-permute-start.4) | collective-permute-done | bytes 688160 | tf_op jit(solution)/shard_map/ppermute | solution.py:386
  32.5 1.3 pad_maximum_fusion
  33.8 2.1 %collective-permute-start.5 = (bf16[4,336,512]{2,1,0:T(8,128)(2,1)}, bf16[4,336,512]{2,1,0:T(8,128)(2,1)}, u32[]{:S(2)}, u32[]{:S(2)}) collective-permute-start(bf16[4,336,512]{2,1,0:T(8,128)(2,1)} %pad_maximum_fusion), channel_id=1, source_target_pairs={{0,1},{1,0},{2,3},{3,2},{4,5},{5,4},{6,7},{7,6},{8,9},{9,8},{10,11... | collective-permute-start | bytes 4128776 | tf_op jit(solution)/shard_map/ppermute | solution.py:386
  35.9 3.3 %collective-permute-start.7 = (s32[2,1024]{1,0:T(2,128)S(1)}, s32[2,1024]{1,0:T(2,128)S(1)}, u32[]{:S(2)}, u32[]{:S(2)}) collective-permute-start(s32[2,1024]{1,0:T(2,128)S(1)} %copy-done.6), channel_id=1, source_target_pairs={{0,16},{16,0},{1,17},{17,1},{2,18},{18,2},{3,19},{19,3},{4,20},{20... | collective-permute-start | bytes 24584 | tf_op jit(solution)/shard_map/ppermute | solution.py:389
  39.6 0.7 reshape.109.gb_ref
  40.3 1.3 constant_dynamic-update-slice_fusion.1
  42.2 1.3 constant_dynamic-update-slice_fusion.x_ref
  43.5 1.3 copy-done
  44.8 3.2 %shard_map.247 = (f32[8,2,2048]{2,1,0:T(2,128)}, f32[8,2,2048]{2,1,0:T(2,128)}) custom-call(s32[8]{0:T(128)} %fusion.3.slot_ref, bf16[2048,512]{1,0:T(8,128)(2,1)} %copy-done, bf16[32,512]{1,0:T(8,128)(2,1)} %bitcast.62, f32[32,1]{1,0:T(8,128)} %reshape.109.gb_ref), custom_call_target="tpu_custom_call" | custom-call | flops 67108864 | bytes 2097152 | tf_op jit(solution)/shard_map/pallas_call | solution.py:69
  48.0 9.7 %shard_map.248 = (bf16[2,256,2048]{2,1,0:T(8,128)(2,1)}, bf16[2,256,2048]{2,1,0:T(8,128)(2,1)}, bf16[2,128,2048]{2,1,0:T(8,128)(2,1)}, bf16[2,128,2048]{2,1,0:T(8,128)(2,1)}, f32[2,128,2048]{2,1,0:T(8,128)}) custom-call(bf16[2048,512]{1,0:T(8,128)(2,1)} %copy-done, bf16[2,336,512]{2,1,0:T(8,128)(2,1)} %copy-done.2, f32[8,2,2048]{2,1,0:T(2,128)} %get-tuple-element.39.low_ref), custom_call_target="tpu_custom_call" | custom-call | flops 1342177280 | bytes 6291456 | tf_op jit(solution)/shard_map/pallas_call | solution.py:132
  57.7 10.2 %shard_map.249 = (bf16[2,256,2048]{2,1,0:T(8,128)(2,1)}, bf16[2,256,2048]{2,1,0:T(8,128)(2,1)}, bf16[2,128,2048]{2,1,0:T(8,128)(2,1)}, bf16[2,128,2048]{2,1,0:T(8,128)(2,1)}, f32[2,128,2048]{2,1,0:T(8,128)}) custom-call(bf16[2048,512]{1,0:T(8,128)(2,1)} %copy-done, bf16[2,336,512]{2,1,0:T(8,128)(2,1)} %copy-done.1, f32[8,2,2048]{2,1,0:T(2,128)} %get-tuple-element.39.low_ref, ...), custom_call_target="tpu_custom_call" | custom-call | flops 1342177280 | bytes 6291456 | tf_op jit(solution)/shard_map/pallas_call | solution.py:132
  68.0 16.2 %shard_map.250 = (bf16[4,256,2048]{2,1,0:T(8,128)(2,1)}, bf16[4,256,2048]{2,1,0:T(8,128)(2,1)}, bf16[4,128,2048]{2,1,0:T(8,128)(2,1)}, bf16[4,128,2048]{2,1,0:T(8,128)(2,1)}, f32[2,128,2048]{2,1,0:T(8,128)}) custom-call(bf16[2048,512]{1,0:T(8,128)(2,1)} %copy-done, bf16[4,336,512]{2,1,0:T(8,128)(2,1)} %collective-permute-done.5.pay_ref.refs_5_, ...), custom_call_target="tpu_custom_call" | custom-call | flops 2684354560 | bytes 12582912 | tf_op jit(solution)/shard_map/pallas_call | solution.py:132
  84.2 1.7 convert_element_type.53
  87.4 0.7 copy.56.tl_ref
  88.1 0.7 copy.55.tb_ref
  89.5 1.0 copy-done.4
  90.4 9.4 %shard_map.251 = (f32[2,2048]{1,0:T(2,128)}, f32[2,128,2048]{2,1,0:T(8,128)}, bf16[32,2048]{1,0:T(8,128)(2,1)}, f32[80,512]{1,0:T(8,128)}) custom-call(s32[8]{0:T(128)} %fusion.3.slot_ref, bf16[2048,512]{1,0:T(8,128)(2,1)} %copy-done, f32[2,128,2048]{2,1,0:T(8,128)} %get-tuple-element.42.mix_ref, bf16[2,128,2048]{2,1,0:T(8,128)(2,1)} %copy-done.4, ...), custom_call_target="tpu_custom_call" | custom-call | flops 201326592 | bytes 8388608 | tf_op jit(solution)/shard_map/pallas_call | solution.py:238
  99.9 10.8 %shard_map.254 = (bf16[4,336,512]{2,1,0:T(8,128)(2,1)}, bf16[4,256,2048]{2,1,0:T(8,128)(2,1)}) custom-call(bf16[2048,512]{1,0:T(8,128)(2,1)} %copy-done, bf16[4,336,512]{2,1,0:T(8,128)(2,1)} %collective-permute-done.5.pay_ref.refs_5_, f32[8,2,2048]{2,1,0:T(2,128)} %get-tuple-element.39.low_ref, f32[2,128,2048]{2,1,0:T(8,128)} %get-tuple-element.49.dmix_ref, ...), custom_call_target="tpu_custom_call" | custom-call | flops 3221225472 | bytes 14745600 | tf_op jit(solution)/shard_map/pallas_call | solution.py:296
  110.7 1.5 collective-permute-start.9
  112.2 7.0 %shard_map.253 = (bf16[2,336,512]{2,1,0:T(8,128)(2,1)}, bf16[2,256,2048]{2,1,0:T(8,128)(2,1)}) custom-call(bf16[2048,512]{1,0:T(8,128)(2,1)} %copy-done, bf16[2,336,512]{2,1,0:T(8,128)(2,1)} %copy-done.1, f32[8,2,2048]{2,1,0:T(2,128)} %get-tuple-element.39.low_ref, f32[2,128,2048]{2,1,0:T(8,128)} %get-tuple-element.49.dmix_ref, ...), custom_call_target="tpu_custom_call" | custom-call | flops 1610612736 | bytes 7372800 | tf_op jit(solution)/shard_map/pallas_call | solution.py:296
  119.2 10.0 %collective-permute-done.9 = bf16[4,336,512]{2,1,0:T(8,128)(2,1)S(1)} collective-permute-done((bf16[4,336,512]{2,1,0:T(8,128)(2,1)}, bf16[4,336,512]{2,1,0:T(8,128)(2,1)S(1)}, u32[]{:S(2)}, u32[]{:S(2)}) %collective-permute-start.9) | collective-permute-done | bytes 1376288 | tf_op jit(solution)/shard_map/ppermute | solution.py:386
  129.2 1.3 add_convert_fusion.1
  131.4 7.0 %shard_map.252 = (bf16[2,336,512]{2,1,0:T(8,128)(2,1)}, bf16[2,256,2048]{2,1,0:T(8,128)(2,1)}) custom-call(bf16[2048,512]{1,0:T(8,128)(2,1)} %copy-done, bf16[2,336,512]{2,1,0:T(8,128)(2,1)} %copy-done.2, f32[8,2,2048]{2,1,0:T(2,128)} %get-tuple-element.39.low_ref, f32[2,128,2048]{2,1,0:T(8,128)} %get-tuple-element.49.dmix_ref, ...), custom_call_target="tpu_custom_call" | custom-call | flops 1610612736 | bytes 7372800 | tf_op jit(solution)/shard_map/pallas_call | solution.py:296
  138.4 12.4 %collective-permute-start.16 = (f32[80,512]{1,0:T(8,128)S(1)}, f32[80,512]{1,0:T(8,128)S(1)}, u32[]{:S(2)}, u32[]{:S(2)}) collective-permute-start(f32[80,512]{1,0:T(8,128)S(1)} %add.78), channel_id=1, source_target_pairs={{0,8},{1,9},{2,10},{3,11},{4,12},{5,13},{6,14},{7,15},{8,0},{9,1},... | collective-permute-start | bytes 491528 | tf_op jit(solution)/shard_map/ppermute | solution.py:386
  150.9 1.4 convert_add_fusion
  153.0 6.4 %collective-permute-done.16 = f32[80,512]{1,0:T(8,128)S(1)} collective-permute-done((f32[80,512]{1,0:T(8,128)S(1)}, f32[80,512]{1,0:T(8,128)S(1)}, u32[]{:S(2)}, u32[]{:S(2)}) %collective-permute-start.16) | collective-permute-done | bytes 163872 | tf_op jit(solution)/shard_map/ppermute | solution.py:386
  159.4 0.7 collective-permute-start.17
  160.1 6.3 %collective-permute-done.17 = f32[80,512]{1,0:T(8,128)S(1)} collective-permute-done((f32[80,512]{1,0:T(8,128)S(1)}, f32[80,512]{1,0:T(8,128)S(1)}, u32[]{:S(2)}, u32[]{:S(2)}) %collective-permute-start.17) | collective-permute-done | bytes 163872 | tf_op jit(solution)/shard_map/ppermute | solution.py:386
  166.6 6.0 %collective-permute-done.18 = f32[80,512]{1,0:T(8,128)S(1)} collective-permute-done((f32[80,512]{1,0:T(8,128)S(1)}, f32[80,512]{1,0:T(8,128)S(1)}, u32[]{:S(2)}, u32[]{:S(2)}) %collective-permute-start.18) | collective-permute-done | bytes 163872 | tf_op jit(solution)/shard_map/ppermute | solution.py:386
  173.2 1.9 collective-permute-start.13
  175.3 1.3 collective-permute-start.12
  176.6 6.5 %shard_map.255 = bf16[1024,512]{1,0:T(8,128)(2,1)} custom-call(bf16[32,2048]{1,0:T(8,128)(2,1)} %get-tuple-element.48.dgate_ref, bf16[32,512]{1,0:T(8,128)(2,1)} %bitcast.63, bf16[2,256,2048]{2,1,0:T(8,128)(2,1)} %get-tuple-element.53.refs_0_, bf16[2,256,2048]{2,1,0:T(8,128)(2,1)} %get-tuple-element.57.refs_1_, ...), custom_call_target="tpu_custom_call" | custom-call | flops 2147483648 | bytes 4194304 | tf_op jit(solution)/shard_map/pallas_call | solution.py:340
  183.7 1.3 collective-permute-start.8
  185.0 4.0 %collective-permute-done.12 = bf16[336,512]{1,0:T(8,128)(2,1)S(1)} collective-permute-done((bf16[336,512]{1,0:T(8,128)(2,1)S(1)}, bf16[336,512]{1,0:T(8,128)(2,1)S(1)}, u32[]{:S(2)}, u32[]{:S(2)}) %collective-permute-start.12) | collective-permute-done | bytes 344096 | tf_op jit(solution)/shard_map/ppermute | solution.py:386
  193.3 1.0 copy-done.3
  194.3 6.9 %shard_map.256 = f32[1024,512]{1,0:T(8,128)} custom-call(bf16[32,2048]{1,0:T(8,128)(2,1)} %get-tuple-element.48.dgate_ref, bf16[32,512]{1,0:T(8,128)(2,1)} %bitcast.64, bf16[2,256,2048]{2,1,0:T(8,128)(2,1)} %get-tuple-element.53.refs_0_, bf16[2,256,2048]{2,1,0:T(8,128)(2,1)} %get-tuple-element.57.refs_1_, bf16[4,256,2048]{2,1,0:T(8,128)(2,1)} %get-tuple-element.61.refs_2_, ...), custom_call_target="tpu_custom_call" | custom-call | flops 2147483648 | bytes 4194304 | tf_op jit(solution)/shard_map/pallas_call | solution.py:340
  202.5 1.0 copy.57
  203.5 0.8 copy.58
  (100 shorter events, 12.7 us)
Async XLA Ops:
  4.1 10.7 %collective-permute-start.1 = (bf16[336,512]{1,0:T(8,128)(2,1)S(1)}, bf16[336,512]{1,0:T(8,128)(2,1)S(1)}, u32[]{:S(2)}, u32[]{:S(2)}) collective-permute-start(bf16[336,512]{1,0:T(8,128)(2,1)S(1)} %pad_maximum_fusion.2), channel_id=1, source_target_pairs={{0,8},{1,9},{2,10},{3,11},{4,12},{5,13},{6,14},{7,15},{24,16},{25,... | collective-permute-start | bytes 1032200 | tf_op jit(solution)/shard_map/ppermute | solution.py:386
  10.1 11.0 %collective-permute-start.2 = (bf16[336,512]{1,0:T(8,128)(2,1)S(1)}, bf16[336,512]{1,0:T(8,128)(2,1)S(1)}, u32[]{:S(2)}, u32[]{:S(2)}) collective-permute-start(bf16[336,512]{1,0:T(8,128)(2,1)S(1)} %pad_maximum_fusion.2), channel_id=1, source_target_pairs={{0,4},{1,5},{2,6},{3,7},{4,0},{5,1},{6,2},{7,3},{24,28},{25,29},{2... | collective-permute-start | bytes 1032200 | tf_op jit(solution)/shard_map/ppermute | solution.py:386
  14.9 6.2 %collective-permute-start.3 = (bf16[336,512]{1,0:T(8,128)(2,1)S(1)}, bf16[336,512]{1,0:T(8,128)(2,1)S(1)}, u32[]{:S(2)}, u32[]{:S(2)}) collective-permute-start(bf16[336,512]{1,0:T(8,128)(2,1)S(1)} %broadcast_select_fusion.1), channel_id=1, source_target_pairs={{8,12},{9,13},{10,14},{11,15},{12,8},{13,9},{14,10},{15,11},{16,20... | collective-permute-start | bytes 1032200 | tf_op jit(solution)/shard_map/ppermute | solution.py:386
  21.3 12.6 %copy-start.2 = (bf16[2,336,512]{2,1,0:T(8,128)(2,1)}, bf16[2,336,512]{2,1,0:T(8,128)(2,1)S(1)}, u32[]{:S(2)}) copy-start(bf16[2,336,512]{2,1,0:T(8,128)(2,1)S(1)} %pad_maximum_fusion.1.pay_ref.refs_3_) | copy-start | bytes 2064388
  21.3 14.6 %copy-start.6 = (s32[2,1024]{1,0:T(2,128)S(1)}, s32[2,1024]{1,0:T(2,128)}, u32[]{:S(2)}) copy-start(s32[2,1024]{1,0:T(2,128)} %param.27) | copy-start | bytes 24580
  21.3 17.9 %copy-start.8 = (s32[16]{0:T(128)S(1)}, s32[16]{0:T(128)}, u32[]{:S(2)}) copy-start(s32[16]{0:T(128)} %param.28) | copy-start | bytes 196
  21.3 17.9 %copy-start.12 = (s32[16]{0:T(128)S(1)}, s32[16]{0:T(128)}, u32[]{:S(2)}) copy-start(s32[16]{0:T(128)} %param.29) | copy-start | bytes 196
  21.3 18.3 %copy-start.9 = (bf16[2,16]{1,0:T(2,128)(2,1)S(1)}, bf16[2,16]{1,0:T(2,128)(2,1)}, u32[]{:S(2)}) copy-start(bf16[2,16]{1,0:T(2,128)(2,1)} %param.22) | copy-start | bytes 196
  21.3 11.2 %collective-permute-start.4 = (bf16[2,336,512]{2,1,0:T(8,128)(2,1)S(1)}, bf16[2,336,512]{2,1,0:T(8,128)(2,1)S(1)}, u32[]{:S(2)}, u32[]{:S(2)}) collective-permute-start(bf16[2,336,512]{2,1,0:T(8,128)(2,1)S(1)} %pad_maximum_fusion.1.pay_ref.refs_3_), channel_id=1, source_target_pairs={{0,2},{1,3},{2,0},{3,1},{4,6},{5,7},{6,4},{7,5},{8,10},{9,11},{10,... | collective-permute-start | bytes 2064392 | tf_op jit(solution)/shard_map/ppermute | solution.py:386
  23.6 18.6 %collective-permute-start = (bf16[1024,512]{1,0:T(8,128)(2,1)}, bf16[1024,512]{1,0:T(8,128)(2,1)}, u32[]{:S(2)}, u32[]{:S(2)}) collective-permute-start(bf16[1024,512]{1,0:T(8,128)(2,1)} %param.16), channel_id=1, source_target_pairs={{0,16},{16,0},{1,17},{17,1},{2,18},{18,2},{3,19},{19,3},{4,20},{20... | collective-permute-start | bytes 3145736 | tf_op jit(solution)/shard_map/ppermute | solution.py:389
  32.5 1.3 copy-start.1
  33.8 7.8 %copy-start.10 = (s32[8]{0:T(128)S(1)}, s32[8]{0:T(128)}, u32[]{:S(2)}) copy-start(s32[8]{0:T(128)} %constant.54.clone) | copy-start | bytes 100
  33.8 7.8 %copy-start.11 = (s32[8]{0:T(128)S(1)}, s32[8]{0:T(128)}, u32[]{:S(2)}) copy-start(s32[8]{0:T(128)} %constant.53.clone) | copy-start | bytes 100
  33.8 34.1 %collective-permute-start.5 = (bf16[4,336,512]{2,1,0:T(8,128)(2,1)}, bf16[4,336,512]{2,1,0:T(8,128)(2,1)}, u32[]{:S(2)}, u32[]{:S(2)}) collective-permute-start(bf16[4,336,512]{2,1,0:T(8,128)(2,1)} %pad_maximum_fusion), channel_id=1, source_target_pairs={{0,1},{1,0},{2,3},{3,2},{4,5},{5,4},{6,7},{7,6},{8,9},{9,8},{10,11... | collective-permute-start | bytes 4128776 | tf_op jit(solution)/shard_map/ppermute | solution.py:386
  35.9 53.0 %collective-permute-start.7 = (s32[2,1024]{1,0:T(2,128)S(1)}, s32[2,1024]{1,0:T(2,128)S(1)}, u32[]{:S(2)}, u32[]{:S(2)}) collective-permute-start(s32[2,1024]{1,0:T(2,128)S(1)} %copy-done.6), channel_id=1, source_target_pairs={{0,16},{16,0},{1,17},{17,1},{2,18},{18,2},{3,19},{19,3},{4,20},{20... | collective-permute-start | bytes 24584 | tf_op jit(solution)/shard_map/ppermute | solution.py:389
  43.5 1.3 copy-start
  84.2 2.0 copy-start.13
  84.2 2.0 copy-start.14
  84.2 2.6 %copy-start.15 = (bf16[2]{0:T(256)(128)(2,1)S(1)}, bf16[2]{0:T(256)(128)(2,1)}, u32[]{:S(2)}) copy-start(bf16[2]{0:T(256)(128)(2,1)} %param.26) | copy-start | bytes 16
  86.0 3.5 %collective-permute-start.6 = (bf16[2,128,2048]{2,1,0:T(8,128)(2,1)S(1)}, bf16[2,128,2048]{2,1,0:T(8,128)(2,1)S(1)}, u32[]{:S(2)}, u32[]{:S(2)}) collective-permute-start(bf16[2,128,2048]{2,1,0:T(8,128)(2,1)S(1)} %convert_element_type.53), channel_id=1, source_target_pairs={{0,16},{16,0},{1,17},{17,1},{2,18},{18,2},{3,19},{19,3},{4,20},{20... | collective-permute-start | bytes 3145736 | tf_op jit(solution)/shard_map/ppermute | solution.py:389
  89.4 1.0 copy-start.4
  110.7 18.5 %collective-permute-start.9 = (bf16[4,336,512]{2,1,0:T(8,128)(2,1)}, bf16[4,336,512]{2,1,0:T(8,128)(2,1)S(1)}, u32[]{:S(2)}, u32[]{:S(2)}) collective-permute-start(bf16[4,336,512]{2,1,0:T(8,128)(2,1)} %get-tuple-element.63), channel_id=1, source_target_pairs={{0,1},{1,0},{2,3},{3,2},{4,5},{5,4},{6,7},{7,6},{8,9},{9,8},{10,11... | collective-permute-start | bytes 4128776 | tf_op jit(solution)/shard_map/ppermute | solution.py:386
  119.2 11.7 %copy-start.5 = (f32[80,512]{1,0:T(8,128)S(1)}, f32[80,512]{1,0:T(8,128)}, u32[]{:S(2)}) copy-start(f32[80,512]{1,0:T(8,128)} %get-tuple-element.65) | copy-start | bytes 491524
  130.5 20.4 %collective-permute-start.10 = (bf16[2,336,512]{2,1,0:T(8,128)(2,1)S(1)}, bf16[2,336,512]{2,1,0:T(8,128)(2,1)S(1)}, u32[]{:S(2)}, u32[]{:S(2)}) collective-permute-start(bf16[2,336,512]{2,1,0:T(8,128)(2,1)S(1)} %add_convert_fusion.1), channel_id=1, source_target_pairs={{0,2},{1,3},{2,0},{3,1},{4,6},{5,7},{6,4},{7,5},{8,10},{9,11},{10,... | collective-permute-start | bytes 2064392 | tf_op jit(solution)/shard_map/ppermute | solution.py:386
  130.9 7.5 %collective-permute-start.15 = (f32[80,512]{1,0:T(8,128)S(1)}, f32[80,512]{1,0:T(8,128)S(1)}, u32[]{:S(2)}, u32[]{:S(2)}) collective-permute-start(f32[80,512]{1,0:T(8,128)S(1)} %copy-done.5), channel_id=1, source_target_pairs={{0,16},{16,0},{1,17},{17,1},{2,18},{18,2},{3,19},{19,3},{4,20},{20... | collective-permute-start | bytes 491528 | tf_op jit(solution)/shard_map/ppermute | solution.py:389
  138.4 20.9 %collective-permute-start.16 = (f32[80,512]{1,0:T(8,128)S(1)}, f32[80,512]{1,0:T(8,128)S(1)}, u32[]{:S(2)}, u32[]{:S(2)}) collective-permute-start(f32[80,512]{1,0:T(8,128)S(1)} %add.78), channel_id=1, source_target_pairs={{0,8},{1,9},{2,10},{3,11},{4,12},{5,13},{6,14},{7,15},{8,0},{9,1},... | collective-permute-start | bytes 491528 | tf_op jit(solution)/shard_map/ppermute | solution.py:386
  152.3 22.9 %collective-permute-start.11 = (bf16[336,512]{1,0:T(8,128)(2,1)S(1)}, bf16[336,512]{1,0:T(8,128)(2,1)S(1)}, u32[]{:S(2)}, u32[]{:S(2)}) collective-permute-start(bf16[336,512]{1,0:T(8,128)(2,1)S(1)} %fusion), channel_id=1, source_target_pairs={{8,12},{9,13},{10,14},{11,15},{12,8},{13,9},{14,10},{15,11},{16,20... | collective-permute-start | bytes 1032200 | tf_op jit(solution)/shard_map/ppermute | solution.py:386
  159.4 7.1 %collective-permute-start.17 = (f32[80,512]{1,0:T(8,128)S(1)}, f32[80,512]{1,0:T(8,128)S(1)}, u32[]{:S(2)}, u32[]{:S(2)}) collective-permute-start(f32[80,512]{1,0:T(8,128)S(1)} %add.79), channel_id=1, source_target_pairs={{0,4},{1,5},{2,6},{3,7},{4,0},{5,1},{6,2},{7,3},{8,12},{9,13},{10,... | collective-permute-start | bytes 491528 | tf_op jit(solution)/shard_map/ppermute | solution.py:386
  166.5 6.1 %collective-permute-start.18 = (f32[80,512]{1,0:T(8,128)S(1)}, f32[80,512]{1,0:T(8,128)S(1)}, u32[]{:S(2)}, u32[]{:S(2)}) collective-permute-start(f32[80,512]{1,0:T(8,128)S(1)} %add.80), channel_id=1, source_target_pairs={{0,2},{1,3},{2,0},{3,1},{4,6},{5,7},{6,4},{7,5},{8,10},{9,11},{10,... | collective-permute-start | bytes 491528 | tf_op jit(solution)/shard_map/ppermute | solution.py:386
  172.6 12.3 %collective-permute-start.19 = (f32[80,512]{1,0:T(8,128)S(1)}, f32[80,512]{1,0:T(8,128)S(1)}, u32[]{:S(2)}, u32[]{:S(2)}) collective-permute-start(f32[80,512]{1,0:T(8,128)S(1)} %add.81), channel_id=1, source_target_pairs={{0,1},{1,0},{2,3},{3,2},{4,5},{5,4},{6,7},{7,6},{8,9},{9,8},{10,11... | collective-permute-start | bytes 491528 | tf_op jit(solution)/shard_map/ppermute | solution.py:386
  173.2 11.8 %collective-permute-start.13 = (bf16[336,512]{1,0:T(8,128)(2,1)S(1)}, bf16[336,512]{1,0:T(8,128)(2,1)S(1)}, u32[]{:S(2)}, u32[]{:S(2)}) collective-permute-start(bf16[336,512]{1,0:T(8,128)(2,1)S(1)} %fusion), channel_id=1, source_target_pairs={{0,4},{1,5},{2,6},{3,7},{4,0},{5,1},{6,2},{7,3},{24,28},{25,29},{2... | collective-permute-start | bytes 1032200 | tf_op jit(solution)/shard_map/ppermute | solution.py:386
  175.3 13.8 %collective-permute-start.12 = (bf16[336,512]{1,0:T(8,128)(2,1)S(1)}, bf16[336,512]{1,0:T(8,128)(2,1)S(1)}, u32[]{:S(2)}, u32[]{:S(2)}) collective-permute-start(bf16[336,512]{1,0:T(8,128)(2,1)S(1)} %add_convert_fusion.2), channel_id=1, source_target_pairs={{8,0},{9,1},{10,2},{11,3},{12,4},{13,5},{14,6},{15,7},{16,24},{17,... | collective-permute-start | bytes 1032200 | tf_op jit(solution)/shard_map/ppermute | solution.py:386
  176.6 6.5 %copy-start.7 = (f32[2,2048]{1,0:T(2,128)S(1)}, f32[2,2048]{1,0:T(2,128)}, u32[]{:S(2)}) copy-start(f32[2,2048]{1,0:T(2,128)} %get-tuple-element.47) | copy-start | bytes 49156
  183.7 9.6 %collective-permute-start.8 = (bf16[1024,512]{1,0:T(8,128)(2,1)}, bf16[1024,512]{1,0:T(8,128)(2,1)S(1)}, u32[]{:S(2)}, u32[]{:S(2)}) collective-permute-start(bf16[1024,512]{1,0:T(8,128)(2,1)} %shard_map.255), channel_id=1, source_target_pairs={{0,16},{16,0},{1,17},{17,1},{2,18},{18,2},{3,19},{19,3},{4,20},{20... | collective-permute-start | bytes 3145736 | tf_op jit(solution)/shard_map/ppermute | solution.py:389
  189.2 12.0 %collective-permute-start.14 = (f32[336,512]{1,0:T(8,128)S(1)}, f32[336,512]{1,0:T(8,128)S(1)}, u32[]{:S(2)}, u32[]{:S(2)}) collective-permute-start(f32[336,512]{1,0:T(8,128)S(1)} %convert_add_fusion.1), channel_id=1, source_target_pairs={{0,16},{16,0},{1,17},{17,1},{2,18},{18,2},{3,19},{19,3},{4,20},{20... | collective-permute-start | bytes 2064392 | tf_op jit(solution)/shard_map/ppermute | solution.py:389
  193.3 1.0 copy-start.3
